TPU v7x, 32 devices: a whole 2x2x4 slice. The times are simulated.
32 devices in a mesh: row: 4 (over y, core), col: 8 (over z, x).
Axes of the slice: x: 2, y: 2, z: 4, core: 2. Of those that a mesh axis runs over, the one named last changes fastest.
Arguments:
- object_amp: float32 [4, 2048, 4096], P(None, 'row', 'col'), may hold values from 0.5 to 1.5
- object_phase: float32 [4, 2048, 4096], P(None, 'row', 'col'), may hold values from -3.140625 to 3.140625
- probe_field: float32 [2, 256, 256], replicated, may hold values from -5 to 5
- measured: float32 [4, 8, 4, 256, 256], P('row', 'col'), may hold values from 0 to 2
- offsets: int32 [4, 8, 4, 2], P('row', 'col'), may hold values from 0 to 512
- counts: int32 [4, 8], P('row', 'col'), may hold values from 1 to 4, as said below
Outputs:
- new_real: float32 [4, 2048, 4096], P(None, 'row', 'col')
- new_imag: float32 [4, 2048, 4096], P(None, 'row', 'col')
Inputs may be any that keep to these rules, and one draw needn't show every extreme that they name: `counts`: every count is at least one, and some tile uses all 4 slots. Slots at or beyond a tile's count are unused. `offsets`: entries of unused slots carry no meaning.
All inputs are finite; a program needn't handle non-finite values.
Results may differ from a plain program's by a relative error of at most 0.0003.
Values sent between devices are 32-bit elements; how exact they have to be, the bound alone decides.
A program may use at most 192 MiB of HBM per device.

v0:
```python
import math

import jax
import jax.numpy as jnp
from jax import lax
from jax.sharding import PartitionSpec as P

FRESNEL = 0.0005
HIGHEST = lax.Precision.HIGHEST


def shifted(value, axis, steps):
    count = lax.axis_size(axis)
    leading, last = (max(0, -steps), min(count, count - steps))
    return lax.ppermute(value, axis, [(source, source + steps) for source in range(leading, last)])


def padded_2(x, sides, width):
    for axis, dim in sides:
        size, length = (lax.axis_size(axis), x.shape[dim])
        up = [(i, (i + 1) % size) for i in range(size - 1)]
        down = [(j, i) for i, j in up]
        last = lax.slice_in_dim(x, length - width, length, axis=dim)
        leading = lax.slice_in_dim(x, 0, width, axis=dim)
        before = lax.ppermute(last, axis, up)
        after = lax.ppermute(leading, axis, down)
        x = jnp.concatenate([before, x, after], axis=dim)
    return x


def dft_tables(extent):
    counter = jnp.arange(extent, dtype=jnp.int32)
    product_mod = counter[:, None] * counter[None, :] % extent
    angles = product_mod.astype(jnp.float32) * (2.0 * math.pi / extent)
    factor = 1.0 / math.sqrt(extent)
    cosine = jnp.cos(angles) * factor
    sine_table = jnp.sin(angles) * factor
    frequency = ((counter + extent // 2) % extent - extent // 2).astype(jnp.float32)
    phases = FRESNEL * (frequency[:, None] ** 2 + frequency[None, :] ** 2)
    return (
        jnp.concatenate([cosine, sine_table], 0),
        jnp.concatenate([cosine, sine_table], 1),
        jnp.cos(phases),
        jnp.sin(phases),
    )


def transform(wave, orient, tables):
    extent = wave[0].shape[0]
    left_part = jnp.dot(tables[0], jnp.concatenate([wave[0], wave[1]], 1), precision=HIGHEST)
    half_real = left_part[:extent, :extent] - orient * left_part[extent:, extent:]
    half_imag = left_part[:extent, extent:] + orient * left_part[extent:, :extent]
    right_part = jnp.dot(jnp.concatenate([half_real, half_imag], 0), tables[1], precision=HIGHEST)
    out_real = right_part[:extent, :extent] - orient * right_part[extent:, extent:]
    out_imag = right_part[extent:, :extent] + orient * right_part[:extent, extent:]
    return (out_real, out_imag)


def product_of(first, second):
    return (
        first[0] * second[0] - first[1] * second[1],
        first[0] * second[1] + first[1] * second[0],
    )


def conj_product(first, second):
    return (
        first[0] * second[0] + first[1] * second[1],
        first[0] * second[1] - first[1] * second[0],
    )


def propagate(wave, orient, tables):
    spectrum = transform(wave, -1.0, tables)
    kernel = (tables[2], orient * tables[3])
    return transform(product_of(spectrum, kernel), 1.0, tables)


def position_terms(window, target, probe_field, tables):
    layers = window.shape[1]
    wave = (probe_field[0], probe_field[1])
    incident = []
    exit_wave = wave
    for layer in range(layers):
        incident.append(wave)
        exit_wave = product_of(wave, (window[0, layer], window[1, layer]))
        if layer + 1 < layers:
            wave = propagate(exit_wave, 1.0, tables)
    far = transform(exit_wave, -1.0, tables)
    misfit = far[0] * far[0] + far[1] * far[1] - target
    back = transform((misfit * far[0], misfit * far[1]), 1.0, tables)
    grads_real = [None] * layers
    grads_imag = [None] * layers
    lights = [None] * layers
    for layer in reversed(range(layers)):
        here = incident[layer]
        grad_part = conj_product(here, back)
        grads_real[layer] = grad_part[0]
        grads_imag[layer] = grad_part[1]
        lights[layer] = here[0] * here[0] + here[1] * here[1]
        if layer > 0:
            slab_part = (window[0, layer], window[1, layer])
            back = propagate(conj_product(slab_part, back), -1.0, tables)
    return jnp.stack([jnp.stack(grads_real), jnp.stack(grads_imag), jnp.stack(lights)])


def add_window(totals, piece, top, left):
    start = (jnp.int32(0), jnp.int32(0), top, left)
    region = lax.dynamic_slice(totals, start, piece.shape)
    return lax.dynamic_update_slice(totals, region + piece, start)


def fold_rows(totals, width):
    upper_rim = totals[:, :, :width, :]
    lower_rim = totals[:, :, -width:, :]
    from_next = shifted(upper_rim, "row", -1)
    from_prev = shifted(lower_rim, "row", 1)
    centre = totals[:, :, width:-width, :]
    centre = centre.at[:, :, :width, :].add(from_prev)
    return centre.at[:, :, -width:, :].add(from_next)


def fold_cols(totals, width):
    upper_rim = totals[:, :, :, :width]
    lower_rim = totals[:, :, :, -width:]
    from_next = shifted(upper_rim, "col", -1)
    from_prev = shifted(lower_rim, "col", 1)
    centre = totals[:, :, :, width:-width]
    centre = centre.at[:, :, :, :width].add(from_prev)
    return centre.at[:, :, :, -width:].add(from_next)


def body(object_amp, object_phase, probe_field, measured, offsets, counts):
    layers = object_amp.shape[0]
    tile_side = object_amp.shape[1]
    extent = probe_field.shape[1]
    width = extent // 2
    tables = dft_tables(extent)
    slab_real = object_amp * jnp.cos(object_phase)
    slab_imag = object_amp * jnp.sin(object_phase)
    padded = padded_2(jnp.stack([slab_real, slab_imag]), (("row", 2), ("col", 3)), width)
    totals = jnp.zeros((3, layers, tile_side + 2 * width, tile_side + 2 * width), jnp.float32)
    own_count = counts[0, 0]

    def window_at(slot_index):
        top = offsets[0, 0, slot_index, 0]
        left = offsets[0, 0, slot_index, 1]
        start = (jnp.int32(0), jnp.int32(0), top, left)
        return (lax.dynamic_slice(padded, start, (2, layers, extent, extent)), top, left)

    def own_step(slot_index, running):
        window, top, left = window_at(slot_index)
        terms = position_terms(window, measured[0, 0, slot_index], probe_field, tables)
        return add_window(running, terms, top, left)

    totals = lax.fori_loop(0, own_count, own_step, totals)
    totals = fold_cols(fold_rows(totals, width), width)
    denominator = totals[2] + 1.0
    new_real = slab_real - totals[0] / denominator
    new_imag = slab_imag - totals[1] / denominator
    return (new_real, new_imag)


def solution(mesh):
    placed = (
        P(None, "row", "col"),
        P(None, "row", "col"),
        P(),
        P("row", "col", None, None, None),
        P("row", "col", None, None),
        P("row", "col"),
    )
    return jax.shard_map(
        body,
        mesh=mesh,
        in_specs=placed,
        out_specs=(P(None, "row", "col"), P(None, "row", "col")),
        check_vma=False,
    )
```

profile of v0, /device:TPU:19, one launch (start us, length us, event | category | flops | bytes accessed | tf_op | source)
XLA Modules:
  0.0 835.4 jit_solution(2225128358779724816)
XLA Ops:
  0.6 16.3 %fusion.224 = (f32[1,4,512,512]{3,2,1,0:T(8,128)S(1)}, f32[1,4,512,512]{3,2,1,0:T(8,128)S(1)}) fusion(f32[4,512,512]{2,1,0:T(8,128)} %param.16, f32[4,512,512]{2,1,0:T(8,128)} %param.17), kind=kLoop, calls=%fused_computation.363 | loop fusion | flops 2097152 | bytes 16777216 | tf_op jit(solution)/shard_map/stack | solution.py:141
  17.5 3.7 collective-permute-start
  21.3 2.1 collective-permute-start.1
  23.3 20.9 %collective-permute-done = f32[2,4,128,512]{3,2,1,0:T(8,128)S(1)} collective-permute-done((f32[2,4,128,512]{3,2,1,0:T(8,128)S(1)}, f32[2,4,128,512]{3,2,1,0:T(8,128)S(1)}, u32[]{:S(2)}, u32[]{:S(2)}) %collective-permute-start) | collective-permute-done | bytes 2097184 | tf_op jit(solution)/shard_map/ppermute | solution.py:25
  44.2 4.9 collective-permute-done.1
  49.1 3.3 pad_maximum_fusion.4
  52.4 3.2 collective-permute-start.2
  55.6 2.1 collective-permute-start.3
  59.9 110.8 %collective-permute-done.2 = f32[2,4,768,128]{3,2,1,0:T(8,128)} collective-permute-done((f32[2,4,768,128]{3,2,1,0:T(8,128)}, f32[2,4,768,128]{3,2,1,0:T(8,128)}, u32[]{:S(2)}, u32[]{:S(2)}) %collective-permute-start.2) | collective-permute-done | bytes 3145760 | tf_op jit(solution)/shard_map/ppermute | solution.py:25
  170.6 11.9 %pad_maximum_fusion = f32[2,4,768,768]{3,2,1,0:T(8,128)} fusion(f32[2,4,768,128]{3,2,1,0:T(8,128)} %collective-permute-done.3, f32[2,4,128,512]{3,2,1,0:T(8,128)} %copy-done.10, f32[1,4,512,512]{3,2,1,0:T(8,128)} %copy-done.4, f32[1,4,512,512]{3,2,1,0:T(8,128)} %copy-done.3, f32[2,4,128,512]{3,2,1,0:T(8,128)S(1)} %copy-done.9, ...), kind=kLoop, calls=%fused_computation.340 | loop fusion | flops 23592960 | bytes 37748736 | tf_op jit(solution)/shard_map/concatenate | solution.py:27
  182.5 12.1 %broadcast_in_dim.2.clone = f32[3,4,768,768]{3,2,1,0:T(8,128)} broadcast(f32[]{:T(128)} %constant.156.clone.1), dimensions={} | broadcast | bytes 28311556 | tf_op jit(solution)/shard_map/broadcast_in_dim | solution.py:142
  194.6 222.0 %while.19 = (s32[]{:T(128)}, f32[3,4,768,768]{3,2,1,0:T(8,128)}, s32[]{:T(128)}, s32[1,1,4,2]{2,3,1,0:T(2,128)S(1)}, f32[2,256,256]{1,2,0:T(8,128)S(1)}, /*index...) while((s32[]{:T(128)}, f32[3,4,768,768]{3,2,1,0:T(8,128)}, ...), condition=%wide.region_1.2_spmd.clone.clone.clone, body=%wide.region_0.1_spmd.clone.clone.clone.sunk | while | flops 22571122688 | bytes 175124928 | solution.py:156
  200.1 3.2 constant_dynamic-slice_fusion.13
  204.0 1.1 copy.86
  205.1 1.8 copy.81
  207.7 1.1 fusion.416
  211.0 1.9 fusion.419
  217.3 1.2 fusion.424
  223.0 1.4 fusion.429
  231.1 1.1 fusion.436
  234.6 1.4 fusion.440
  240.6 1.2 fusion.445
  246.4 1.5 fusion.450
  249.0 1.1 fusion.451
  250.3 1.2 maximum_bitcast_fusion.5
  251.4 5.0 constant_dynamic-slice_fusion.12
  256.4 3.5 copy.78
  259.9 4.2 maximum_add_fusion.2
  264.2 3.5 copy.87
  267.7 34.3 %dynamic_update_slice.9 = f32[3,4,768,768]{3,2,1,0:T(8,128)} dynamic-update-slice(f32[3,4,768,768]{3,2,1,0:T(8,128)} %get-tuple-element.767, f32[3,4,256,256]{3,2,1,0:T(8,128)} %copy.87, s32[]{:T(128)} %constant.155.clone.1..sunk, s32[]{:T(128)} %constant.155.clone.1..sunk, s32[]{:T(128)S(6)} %select_n.125, s32[]{:T(128)S(6)} %select_n.126) | dynamic-update-slice | bytes 6291460 | tf_op jit(solution)/shard_map/while/body/dynamic_update_slice | solution.py:110
  307.8 3.2 constant_dynamic-slice_fusion.13
  311.7 1.1 copy.86
  312.8 1.8 copy.81
  315.4 1.1 fusion.416
  318.7 1.4 fusion.419
  324.6 1.2 fusion.424
  330.3 1.4 fusion.429
  341.8 1.5 fusion.440
  347.9 1.2 fusion.445
  353.7 1.7 fusion.450
  356.5 1.1 fusion.451
  357.8 1.2 maximum_bitcast_fusion.5
  358.9 5.0 constant_dynamic-slice_fusion.12
  363.9 3.5 copy.78
  367.4 4.2 maximum_add_fusion.2
  371.7 3.5 copy.87
  375.2 34.3 %dynamic_update_slice.9 = f32[3,4,768,768]{3,2,1,0:T(8,128)} dynamic-update-slice(f32[3,4,768,768]{3,2,1,0:T(8,128)} %get-tuple-element.767, f32[3,4,256,256]{3,2,1,0:T(8,128)} %copy.87, s32[]{:T(128)} %constant.155.clone.1..sunk, s32[]{:T(128)} %constant.155.clone.1..sunk, s32[]{:T(128)S(6)} %select_n.125, s32[]{:T(128)S(6)} %select_n.126) | dynamic-update-slice | bytes 6291460 | tf_op jit(solution)/shard_map/while/body/dynamic_update_slice | solution.py:110
  416.6 8.4 %fusion.237 = (f32[3,4,128,768]{3,2,1,0:T(8,128)}, f32[3,4,128,768]{3,2,1,0:T(8,128)}) fusion(f32[3,4,768,768]{3,2,1,0:T(8,128)} %get-tuple-element.252), kind=kLoop, calls=%fused_computation.388 | loop fusion | bytes 18874368 | tf_op jit(solution)/shard_map/slice | solution.py:114
  425.0 1.9 collective-permute-start.4
  426.9 4.5 collective-permute-start.5
  431.4 7.1 slice.785
  438.6 39.7 %collective-permute-done.4 = f32[3,4,128,768]{3,2,1,0:T(8,128)} collective-permute-done((f32[3,4,128,768]{3,2,1,0:T(8,128)}, f32[3,4,128,768]{3,2,1,0:T(8,128)}, u32[]{:S(2)}, u32[]{:S(2)}) %collective-permute-start.4) | collective-permute-done | bytes 4718624 | tf_op jit(solution)/shard_map/ppermute | solution.py:15
  478.2 4.4 add_dynamic-update-slice_fusion
  482.6 1.2 fusion.217
  483.8 6.4 copy-done
  490.2 2.1 fusion.238
  492.3 104.6 %collective-permute-start.6 = (f32[3,4,512,128]{3,2,1,0:T(8,128)}, f32[3,4,512,128]{3,2,1,0:T(8,128)}, u32[]{:S(2)}, u32[]{:S(2)}) collective-permute-start(f32[3,4,512,128]{3,2,1,0:T(8,128)} %get-tuple-element.491), channel_id=1, source_target_pairs={{0,1},{1,2},{2,3},{3,4},{4,5},{5,6},{6,7},{8,9},{9,10},{10,11},{11... | collective-permute-start | bytes 9437192 | tf_op jit(solution)/shard_map/ppermute | solution.py:15
  596.9 114.7 %collective-permute-start.7 = (f32[3,4,512,128]{3,2,1,0:T(8,128)S(1)}, f32[3,4,512,128]{3,2,1,0:T(8,128)}, u32[]{:S(2)}, u32[]{:S(2)}) collective-permute-start(f32[3,4,512,128]{3,2,1,0:T(8,128)S(1)} %get-tuple-element.490), channel_id=1, source_target_pairs={{1,0},{2,1},{3,2},{4,3},{5,4},{6,5},{7,6},{9,8},{10,9},{11,10},{12... | collective-permute-start | bytes 9437192 | tf_op jit(solution)/shard_map/ppermute | solution.py:15
  711.6 10.9 %slice.1279 = f32[3,4,512,512]{3,2,1,0:T(8,128)} slice(f32[3,4,512,768]{3,2,1,0:T(8,128)} %copy-done), slice={[0:3], [0:4], [0:512], [128:640]} | slice | bytes 25165824 | tf_op jit(solution)/shard_map/slice | solution.py:128
  722.6 83.0 %collective-permute-done.6 = f32[3,4,512,128]{3,2,1,0:T(8,128)} collective-permute-done((f32[3,4,512,128]{3,2,1,0:T(8,128)}, f32[3,4,512,128]{3,2,1,0:T(8,128)}, u32[]{:S(2)}, u32[]{:S(2)}) %collective-permute-start.6) | collective-permute-done | bytes 3145760 | tf_op jit(solution)/shard_map/ppermute | solution.py:15
  805.5 5.0 fusion.223
  810.5 5.1 fusion.222
  815.6 1.4 copy-done.6
  817.0 18.1 %fusion.219 = (f32[4,512,512]{2,1,0:T(8,128)}, f32[4,512,512]{2,1,0:T(8,128)}) fusion(f32[3,4,512,512]{3,2,1,0:T(8,128)} %fusion.222, f32[4,512,512]{2,1,0:T(8,128)S(1)} %copy-done.5, f32[4,512,512]{2,1,0:T(8,128)S(1)} %copy-done.6), kind=kLoop, calls=%fused_computation.346 | loop fusion | flops 7340032 | bytes 29360128 | tf_op jit(solution)/shard_map/sub | solution.py:160
  (165 shorter events, 68.7 us)
Async XLA Ops:
  16.9 32.2 %copy-start.3 = (f32[1,4,512,512]{3,2,1,0:T(8,128)}, f32[1,4,512,512]{3,2,1,0:T(8,128)S(1)}, u32[]{:S(2)}) copy-start(f32[1,4,512,512]{3,2,1,0:T(8,128)S(1)} %get-tuple-element.496) | copy-start | bytes 12582916
  16.9 32.2 %copy-start.4 = (f32[1,4,512,512]{3,2,1,0:T(8,128)}, f32[1,4,512,512]{3,2,1,0:T(8,128)S(1)}, u32[]{:S(2)}) copy-start(f32[1,4,512,512]{3,2,1,0:T(8,128)S(1)} %get-tuple-element.497) | copy-start | bytes 12582916
  17.5 26.7 %collective-permute-start = (f32[2,4,128,512]{3,2,1,0:T(8,128)S(1)}, f32[2,4,128,512]{3,2,1,0:T(8,128)S(1)}, u32[]{:S(2)}, u32[]{:S(2)}) collective-permute-start(f32[2,4,128,512]{3,2,1,0:T(8,128)S(1)} %get-tuple-element.494), channel_id=1, source_target_pairs={{0,8},{8,16},{16,24},{1,9},{9,17},{17,25},{2,10},{10,18},{18,26},{... | collective-permute-start | bytes 6291464 | tf_op jit(solution)/shard_map/ppermute | solution.py:25
  21.2 36.5 %copy-start.11 = (f32[2,256,256]{2,1,0:T(8,128)S(1)}, f32[2,256,256]{2,1,0:T(8,128)}, u32[]{:S(2)}) copy-start(f32[2,256,256]{2,1,0:T(8,128)} %param.18) | copy-start | bytes 1572868
  21.3 27.9 %collective-permute-start.1 = (f32[2,4,128,512]{3,2,1,0:T(8,128)S(1)}, f32[2,4,128,512]{3,2,1,0:T(8,128)S(1)}, u32[]{:S(2)}, u32[]{:S(2)}) collective-permute-start(f32[2,4,128,512]{3,2,1,0:T(8,128)S(1)} %get-tuple-element.495), channel_id=1, source_target_pairs={{8,0},{16,8},{24,16},{9,1},{17,9},{25,17},{10,2},{18,10},{26,18},{... | collective-permute-start | bytes 6291464 | tf_op jit(solution)/shard_map/ppermute | solution.py:26
  44.2 8.2 copy-start.8
  49.1 3.3 copy-start.10
  52.4 118.2 %collective-permute-start.2 = (f32[2,4,768,128]{3,2,1,0:T(8,128)}, f32[2,4,768,128]{3,2,1,0:T(8,128)}, u32[]{:S(2)}, u32[]{:S(2)}) collective-permute-start(f32[2,4,768,128]{3,2,1,0:T(8,128)} %get-tuple-element.492), channel_id=1, source_target_pairs={{0,1},{1,2},{2,3},{3,4},{4,5},{5,6},{6,7},{8,9},{9,10},{10,11},{11... | collective-permute-start | bytes 9437192 | tf_op jit(solution)/shard_map/ppermute | solution.py:25
  55.6 115.0 %collective-permute-start.3 = (f32[2,4,768,128]{3,2,1,0:T(8,128)}, f32[2,4,768,128]{3,2,1,0:T(8,128)}, u32[]{:S(2)}, u32[]{:S(2)}) collective-permute-start(f32[2,4,768,128]{3,2,1,0:T(8,128)} %get-tuple-element.493), channel_id=1, source_target_pairs={{1,0},{2,1},{3,2},{4,3},{5,4},{6,5},{7,6},{9,8},{10,9},{11,10},{12... | collective-permute-start | bytes 9437192 | tf_op jit(solution)/shard_map/ppermute | solution.py:26
  57.9 112.7 %copy-start.9 = (f32[2,4,128,512]{3,2,1,0:T(8,128)S(1)}, f32[2,4,128,512]{3,2,1,0:T(8,128)}, u32[]{:S(2)}) copy-start(f32[2,4,128,512]{3,2,1,0:T(8,128)} %copy-done.8) | copy-start | bytes 6291460
  182.5 12.1 %copy-start.12 = (s32[1,1,4,2]{2,3,1,0:T(2,128)S(1)}, s32[1,1,4,2]{2,3,1,0:T(2,128)}, u32[]{:S(2)}) copy-start(s32[1,1,4,2]{2,3,1,0:T(2,128)} %param.20) | copy-start | bytes 100
  195.5 54.5 %copy-start.1 = (f32[2,256,256]{1,2,0:T(8,128)}, f32[2,256,256]{1,2,0:T(8,128)S(1)}, u32[]{:S(2)}) copy-start(f32[2,256,256]{1,2,0:T(8,128)S(1)} %get-tuple-element.788) | copy-start | bytes 1572868 | tf_op jit(solution)/shard_map/while
  248.9 1.4 copy-start.7
  267.7 34.3 %copy-start.2 = (f32[2,256,256]{1,2,0:T(8,128)S(1)}, f32[2,256,256]{1,2,0:T(8,128)}, u32[]{:S(2)}) copy-start(f32[2,256,256]{1,2,0:T(8,128)} %copy-done.1) | copy-start | bytes 1572868 | tf_op jit(solution)/shard_map/while
  303.2 54.4 %copy-start.1 = (f32[2,256,256]{1,2,0:T(8,128)}, f32[2,256,256]{1,2,0:T(8,128)S(1)}, u32[]{:S(2)}) copy-start(f32[2,256,256]{1,2,0:T(8,128)S(1)} %get-tuple-element.788) | copy-start | bytes 1572868 | tf_op jit(solution)/shard_map/while
  356.4 1.4 copy-start.7
  375.2 34.3 %copy-start.2 = (f32[2,256,256]{1,2,0:T(8,128)S(1)}, f32[2,256,256]{1,2,0:T(8,128)}, u32[]{:S(2)}) copy-start(f32[2,256,256]{1,2,0:T(8,128)} %copy-done.1) | copy-start | bytes 1572868 | tf_op jit(solution)/shard_map/while
  425.0 53.3 %collective-permute-start.4 = (f32[3,4,128,768]{3,2,1,0:T(8,128)}, f32[3,4,128,768]{3,2,1,0:T(8,128)}, u32[]{:S(2)}, u32[]{:S(2)}) collective-permute-start(f32[3,4,128,768]{3,2,1,0:T(8,128)} %get-tuple-element.487), channel_id=1, source_target_pairs={{0,8},{8,16},{16,24},{1,9},{9,17},{17,25},{2,10},{10,18},{18,26},{... | collective-permute-start | bytes 14155784 | tf_op jit(solution)/shard_map/ppermute | solution.py:15
  426.9 55.7 %collective-permute-start.5 = (f32[3,4,128,768]{3,2,1,0:T(8,128)}, f32[3,4,128,768]{3,2,1,0:T(8,128)S(1)}, u32[]{:S(2)}, u32[]{:S(2)}) collective-permute-start(f32[3,4,128,768]{3,2,1,0:T(8,128)} %get-tuple-element.486), channel_id=1, source_target_pairs={{8,0},{16,8},{24,16},{9,1},{17,9},{25,17},{10,2},{18,10},{26,18},{... | collective-permute-start | bytes 14155784 | tf_op jit(solution)/shard_map/ppermute | solution.py:15
  483.8 6.4 copy-start
  492.3 313.2 %collective-permute-start.6 = (f32[3,4,512,128]{3,2,1,0:T(8,128)}, f32[3,4,512,128]{3,2,1,0:T(8,128)}, u32[]{:S(2)}, u32[]{:S(2)}) collective-permute-start(f32[3,4,512,128]{3,2,1,0:T(8,128)} %get-tuple-element.491), channel_id=1, source_target_pairs={{0,1},{1,2},{2,3},{3,4},{4,5},{5,6},{6,7},{8,9},{9,10},{10,11},{11... | collective-permute-start | bytes 9437192 | tf_op jit(solution)/shard_map/ppermute | solution.py:15
  596.9 213.6 %collective-permute-start.7 = (f32[3,4,512,128]{3,2,1,0:T(8,128)S(1)}, f32[3,4,512,128]{3,2,1,0:T(8,128)}, u32[]{:S(2)}, u32[]{:S(2)}) collective-permute-start(f32[3,4,512,128]{3,2,1,0:T(8,128)S(1)} %get-tuple-element.490), channel_id=1, source_target_pairs={{1,0},{2,1},{3,2},{4,3},{5,4},{6,5},{7,6},{9,8},{10,9},{11,10},{12... | collective-permute-start | bytes 9437192 | tf_op jit(solution)/shard_map/ppermute | solution.py:15
  810.5 5.1 copy-start.5
  810.5 6.5 copy-start.6
where the time goes:
time: 847 us; the launch traced here: 835 us
  waiting for transfers between devices  259 us (31%)
  starting transfers between devices  237 us (28%)
  local copies, waits for them, and re-layouts  158 us (19%)
  other arithmetic  104 us (12%)
  matrix products  58.2 us (7%)
  loops' own time  18.1 us (2%)
    ppermute x4, starting transfers between devices, shifted(): lax.ppermute(value, axis, [(source, source + steps) for source in range(l...  226 us
    ppermute x2, waiting for transfers between devices, padded_2(): before = lax.ppermute(last, axis, up)  132 us
    ppermute x4, waiting for transfers between devices, shifted(): lax.ppermute(value, axis, [(source, source + steps) for source in range(l...  123 us
    dynamic_update_slice x4, local copies, waits for them, and re-layouts, add_window(): return lax.dynamic_update_slice(totals, region + piece, start)  75.7 us
    dot_general x28, matrix products, transform(): jnp.dot(tables[0], jnp.concatenate([wave[0], wave[1]], 1), precision=HIGH...  29.2 us
    dot_general x28, matrix products, transform(): jnp.dot(jnp.concatenate([half_real, half_imag], 0), tables[1], precision=...  29 us
    sub x20, other arithmetic, product_of(): first[0] * second[0] - first[1] * second[1]  19.6 us
    sub x1, other arithmetic, body(): new_imag = slab_imag - totals[1] / denominator  18.1 us
  transfers between devices with their start and end apart: 8, of which 5 were waited for; matrix products, arithmetic and copies ran while one was open for 4% of the time, Pallas kernels for 0%

commit v1 on v0

v1 whole, which is shorter than its diff:
```python
import functools
import math

import jax
import jax.numpy as jnp
import numpy as np
import ml_dtypes
from jax import lax
from jax.experimental import pallas as pl
from jax.experimental.pallas import tpu as pltpu
from jax.sharding import PartitionSpec as P

FRESNEL = 0.0005
LANES = 128
SUBLANES = 8
VMEM_BYTES = 50 * 1024 * 1024


def shifted(value, axis, steps):
    count = lax.axis_size(axis)
    first, last = (max(0, -steps), min(count, count - steps))
    return lax.ppermute(value, axis, [(source, source + steps) for source in range(first, last)])


def sine_cosine(angle):
    half = angle * 0.5
    square = half * half
    sine = 1.0 / 6227020800.0
    for order in (11, 9, 7, 5, 3, 1):
        sign = -1.0 if (order // 2) % 2 else 1.0
        sine = sine * square + sign / math.factorial(order)
    sine = sine * half
    cosine = -1.0 / math.factorial(14)
    for order in (12, 10, 8, 6, 4, 2, 0):
        sign = -1.0 if (order // 2) % 2 else 1.0
        cosine = cosine * square + sign / math.factorial(order)
    return 2.0 * sine * cosine, 1.0 - 2.0 * sine * sine


def halves(table):
    high = table.astype(ml_dtypes.bfloat16)
    low = (table - high.astype(np.float64)).astype(ml_dtypes.bfloat16)
    return high, low


def make_tables(extent):
    half = extent // 2
    inner = np.arange(half)
    lefts, rights = [], []
    for parity in (0, 1):
        turn = np.outer(2 * inner + parity, inner) % extent
        wave = np.exp(-2j * np.pi * turn / extent) / math.sqrt(extent)
        block = np.block([[wave.real, -wave.imag], [wave.imag, wave.real]])
        for table in (block, block.T):
            high, low = halves(table)
            lefts.append(np.concatenate([high, high, low], 1))
            rights.append(np.concatenate([high, high, low], 0))
    order = np.concatenate([np.arange(0, extent, 2), np.arange(1, extent, 2)])
    frequency = ((order + half) % extent - half).astype(np.float64)
    phases = FRESNEL * (frequency[:, None] ** 2 + frequency[None, :] ** 2)
    fresnel = np.stack([np.cos(phases), np.sin(phases)]).astype(np.float32)
    pick = np.zeros((extent, extent), np.float32)
    pick[order, np.arange(extent)] = 1.0
    pick = np.stack([pick, pick.T]).astype(ml_dtypes.bfloat16)
    return np.stack(lefts), np.stack(rights), fresnel, pick


def split(value):
    high = value.astype(jnp.bfloat16)
    return high, (value - high.astype(jnp.float32)).astype(jnp.bfloat16)


def dot_left(table, value):
    high, low = split(value)
    return jnp.dot(table, jnp.concatenate([high, low, high], 0), preferred_element_type=jnp.float32)


def dot_right(value, table):
    high, low = split(value)
    return jnp.dot(jnp.concatenate([high, low, high], 1), table, preferred_element_type=jnp.float32)


def pieces(value):
    high, rest = split(value)
    low = (value - high.astype(jnp.float32)) - rest.astype(jnp.float32)
    return high, rest, low.astype(jnp.bfloat16)


def permuted(value, pick):
    value = sum(jnp.dot(piece, pick[0], preferred_element_type=jnp.float32) for piece in pieces(value))
    return sum(jnp.dot(pick[1], piece, preferred_element_type=jnp.float32) for piece in pieces(value))


def forward(wave, left, right):
    real, imag = wave
    h = real.shape[0] // 2
    even = dot_left(left[0], jnp.concatenate([real[:h] + real[h:], imag[:h] + imag[h:]], 0))
    odd = dot_left(left[2], jnp.concatenate([real[:h] - real[h:], imag[:h] - imag[h:]], 0))
    real = jnp.concatenate([even[:h], odd[:h]], 0)
    imag = jnp.concatenate([even[h:], odd[h:]], 0)
    even = dot_right(jnp.concatenate([real[:, :h] + real[:, h:], imag[:, :h] + imag[:, h:]], 1), right[1])
    odd = dot_right(jnp.concatenate([real[:, :h] - real[:, h:], imag[:, :h] - imag[:, h:]], 1), right[3])
    return (jnp.concatenate([even[:, :h], odd[:, :h]], 1), jnp.concatenate([even[:, h:], odd[:, h:]], 1))


def inverse(wave, left, right):
    real, imag = wave
    h = real.shape[0] // 2
    even = dot_right(jnp.concatenate([real[:, :h], imag[:, :h]], 1), right[0])
    odd = dot_right(jnp.concatenate([real[:, h:], imag[:, h:]], 1), right[2])
    total, other = even + odd, even - odd
    real = jnp.concatenate([total[:, :h], other[:, :h]], 1)
    imag = jnp.concatenate([total[:, h:], other[:, h:]], 1)
    even = dot_left(left[1], jnp.concatenate([real[:h], imag[:h]], 0))
    odd = dot_left(left[3], jnp.concatenate([real[h:], imag[h:]], 0))
    total, other = even + odd, even - odd
    return (jnp.concatenate([total[:h], other[:h]], 0), jnp.concatenate([total[h:], other[h:]], 0))


def product_of(first, second):
    return (
        first[0] * second[0] - first[1] * second[1],
        first[0] * second[1] + first[1] * second[0],
    )


def conj_product(first, second):
    return (
        first[0] * second[0] + first[1] * second[1],
        first[0] * second[1] - first[1] * second[0],
    )


def place(offset_ref, slot, side, extent):
    spot = []
    for axis, unit in ((0, SUBLANES), (1, LANES)):
        start = offset_ref[slot, axis]
        base = jnp.minimum(start // unit * unit, side - extent - unit)
        spot += [pl.multiple_of(base, unit), start - base]
    return spot


def window_of(padded_ref, plane, spot, extent):
    top, down, base, shift = spot
    wide = padded_ref[plane, pl.ds(top, extent + SUBLANES), pl.ds(base, extent + LANES)]
    wide = pltpu.roll(wide, extent + LANES - shift, 1)[:, :extent]
    return pltpu.roll(wide, extent + SUBLANES - down, 0)[:extent]


def add_window(total_ref, plane, spot, piece):
    top, down, base, shift = spot
    extent = piece.shape[0]
    wide = jnp.concatenate([piece, jnp.zeros((SUBLANES, extent), jnp.float32)], 0)
    wide = pltpu.roll(wide, down, 0)
    wide = jnp.concatenate([wide, jnp.zeros((extent + SUBLANES, LANES), jnp.float32)], 1)
    total_ref[plane, pl.ds(top, extent + SUBLANES), pl.ds(base, extent + LANES)] += pltpu.roll(wide, shift, 1)


def light_of(wave):
    return wave[0] * wave[0] + wave[1] * wave[1]


def clear_first(slot, total_ref):
    @pl.when(slot == 0)
    def _():
        total_ref[...] = jnp.zeros_like(total_ref)


def forward_kernel(offset_ref, count_ref, padded_ref, wave_ref, left, right, fresnel, next_ref, window_ref, light_ref):
    slot = pl.program_id(0)
    clear_first(slot, light_ref)

    @pl.when(slot < count_ref[0])
    def _():
        extent = wave_ref.shape[-1]
        spot = place(offset_ref, slot, padded_ref.shape[-1], extent)
        wave = (wave_ref[0, 0], wave_ref[0, 1])
        window = (window_of(padded_ref, 0, spot, extent), window_of(padded_ref, 1, spot, extent))
        window_ref[0, 0] = window[0]
        window_ref[0, 1] = window[1]
        add_window(light_ref, 0, spot, light_of(wave))
        spectrum = forward(product_of(wave, window), left, right)
        after = inverse(product_of(spectrum, (fresnel[0], fresnel[1])), left, right)
        next_ref[0, 0] = after[0]
        next_ref[0, 1] = after[1]


def middle_kernel(offset_ref, count_ref, padded_ref, wave_ref, measured_ref, left, right, fresnel, pick, back_ref, total_ref):
    slot = pl.program_id(0)
    clear_first(slot, total_ref)

    @pl.when(slot < count_ref[0])
    def _():
        extent = wave_ref.shape[-1]
        h = extent // 2
        spot = place(offset_ref, slot, padded_ref.shape[-1], extent)
        wave = (wave_ref[0, 0], wave_ref[0, 1])
        window = (window_of(padded_ref, 0, spot, extent), window_of(padded_ref, 1, spot, extent))
        add_window(total_ref, 2, spot, light_of(wave))
        far = forward(product_of(wave, window), left, right)
        target = permuted(measured_ref[0], pick)
        misfit = light_of(far) - target
        back = inverse((misfit * far[0], misfit * far[1]), left, right)
        grad = conj_product(wave, back)
        add_window(total_ref, 0, spot, grad[0])
        add_window(total_ref, 1, spot, grad[1])
        spectrum = forward(conj_product(window, back), left, right)
        back = inverse(conj_product((fresnel[0], fresnel[1]), spectrum), left, right)
        back_ref[0, 0] = back[0]
        back_ref[0, 1] = back[1]


def backward_kernel(offset_ref, count_ref, wave_ref, window_ref, back_in, left, right, fresnel, back_ref, total_ref):
    slot = pl.program_id(0)
    clear_first(slot, total_ref)

    @pl.when(slot < count_ref[0])
    def _():
        extent = wave_ref.shape[-1]
        spot = place(offset_ref, slot, total_ref.shape[-1], extent)
        wave = (wave_ref[0, 0], wave_ref[0, 1])
        back = (back_in[0, 0], back_in[0, 1])
        grad = conj_product(wave, back)
        add_window(total_ref, 0, spot, grad[0])
        add_window(total_ref, 1, spot, grad[1])
        if back_ref is not None:
            spectrum = forward(conj_product((window_ref[0, 0], window_ref[0, 1]), back), left, right)
            back = inverse(conj_product((fresnel[0], fresnel[1]), spectrum), left, right)
            back_ref[0, 0] = back[0]
            back_ref[0, 1] = back[1]


def last_kernel(offset_ref, count_ref, wave_ref, back_in, total_ref):
    backward_kernel(offset_ref, count_ref, wave_ref, None, back_in, None, None, None, None, total_ref)


def body(object_amp, object_phase, probe_field, measured, offsets, counts):
    layers, tile_side = object_amp.shape[0], object_amp.shape[1]
    extent = probe_field.shape[1]
    slots = measured.shape[2]
    width = extent // 2
    side = tile_side + 2 * width
    left, right, fresnel, pick = (jnp.asarray(table) for table in make_tables(extent))

    def whole(array):
        return pl.BlockSpec(array.shape, lambda s, *_: (0,) * array.ndim)

    def per_slot(array):
        if array.shape[0] == 1:
            return whole(array)
        return pl.BlockSpec((1,) + array.shape[1:], lambda s, *_: (s,) + (0,) * (array.ndim - 1))

    waves = jax.ShapeDtypeStruct((slots, 2, extent, extent), jnp.float32)

    def planes(count):
        return jax.ShapeDtypeStruct((count, side, side), jnp.float32)

    def call(kernel, ins, outs, transforms):
        flops = transforms * slots * 2 * 4 * 3 * extent**3
        moved = sum(4 * math.prod(x.shape) for x in [a for a, _ in ins] + [a for a, _ in outs])
        return pl.pallas_call(
            kernel,
            grid_spec=pltpu.PrefetchScalarGridSpec(
                num_scalar_prefetch=2,
                grid=(slots,),
                in_specs=[spec(array) for array, spec in ins],
                out_specs=[spec(array) for array, spec in outs],
            ),
            out_shape=[array for array, _ in outs],
            compiler_params=pltpu.CompilerParams(vmem_limit_bytes=VMEM_BYTES, dimension_semantics=("arbitrary",)),
            cost_estimate=pl.CostEstimate(flops=flops, bytes_accessed=moved, transcendentals=0),
        )(offsets[0, 0], counts[0], *[array for array, _ in ins])

    tables = [(left, whole), (right, whole), (fresnel, whole)]

    sine, cosine = sine_cosine(object_phase)
    slab_real, slab_imag = object_amp * cosine, object_amp * sine

    def halo(layer):
        tile = jnp.stack([slab_real[layer], slab_imag[layer]])
        before = shifted(tile[:, :, -width:], "col", 1)
        after = shifted(tile[:, :, :width], "col", -1)
        tile = jnp.concatenate([before, tile, after], 2)
        above = shifted(tile[:, -width:], "row", 1)
        below = shifted(tile[:, :width], "row", -1)
        return jnp.concatenate([above, tile, below], 1)

    def fold(totals):
        from_next = shifted(totals[:, :width], "row", -1)
        from_prev = shifted(totals[:, -width:], "row", 1)
        rest = tile_side - width
        centre = totals[:, width:-width]
        centre = centre + jnp.pad(from_prev, ((0, 0), (0, rest), (0, 0))) + jnp.pad(from_next, ((0, 0), (rest, 0), (0, 0)))
        from_next = shifted(centre[:, :, :width], "col", -1)
        from_prev = shifted(centre[:, :, -width:], "col", 1)
        centre = centre[:, :, width:-width]
        return centre + jnp.pad(from_prev, ((0, 0), (0, 0), (0, rest))) + jnp.pad(from_next, ((0, 0), (0, 0), (rest, 0)))

    padded = [halo(layer) for layer in range(layers)]
    wave = probe_field[None]
    incident, windows, lights = [], [], []
    for layer in range(layers - 1):
        incident.append(wave)
        wave, window, light = call(
            forward_kernel,
            [(padded[layer], whole), (wave, per_slot)] + tables,
            [(waves, per_slot), (waves, per_slot), (planes(1), whole)],
            2,
        )
        windows.append(window)
        lights.append(fold(light)[0])
    back, total = call(
        middle_kernel,
        [(padded[-1], whole), (wave, per_slot), (measured[0, 0], per_slot)] + tables + [(pick, whole)],
        [(waves, per_slot), (planes(3), whole)],
        4,
    )
    total = fold(total)
    lights.append(total[2])
    grads = [total[:2]]
    for layer in reversed(range(layers - 1)):
        if layer > 0:
            back, total = call(
                backward_kernel,
                [(incident[layer], per_slot), (windows[layer], per_slot), (back, per_slot)] + tables,
                [(waves, per_slot), (planes(2), whole)],
                2,
            )
        else:
            (total,) = call(last_kernel, [(incident[0], per_slot), (back, per_slot)], [(planes(2), whole)], 0)
        grads.insert(0, fold(total))
    new_real = [slab_real[s] - grads[s][0] / (lights[s] + 1.0) for s in range(layers)]
    new_imag = [slab_imag[s] - grads[s][1] / (lights[s] + 1.0) for s in range(layers)]
    return (jnp.stack(new_real), jnp.stack(new_imag))


def solution(mesh):
    placed = (
        P(None, "row", "col"),
        P(None, "row", "col"),
        P(),
        P("row", "col", None, None, None),
        P("row", "col", None, None),
        P("row", "col"),
    )
    return jax.shard_map(
        body,
        mesh=mesh,
        in_specs=placed,
        out_specs=(P(None, "row", "col"), P(None, "row", "col")),
        check_vma=False,
    )
```

time: 847 us -> 446 us (0.53)
  local copies, waits for them, and re-layouts: 158 us -> 27.8 us
  waiting for transfers between devices: 259 us -> 142 us
  starting transfers between devices: 237 us -> 145 us
  Pallas kernels: 0 us -> 60.8 us
  matrix products: 58.2 us -> 0 us
  other arithmetic: 104 us -> 60.3 us
  loops' own time: 18.1 us -> 0 us
    ppermute x8 -> x44, waiting for transfers between devices: 259 us -> 142 us  [shifted(): lax.ppermute(value, axis, [(source, source + steps) for source in range(f...]
    ppermute x8 -> x44, starting transfers between devices: 237 us -> 145 us  [shifted(): lax.ppermute(value, axis, [(source, source + steps) for source in range(f...]
    dynamic_update_slice x4 -> x0, local copies, waits for them, and re-layouts: 75.7 us -> none  [add_window(): return lax.dynamic_update_slice(totals, region + piece, start)]
    pallas_call x0 -> x7, Pallas kernels: none -> 60.8 us  [call(): pl.pallas_call(kernel, grid_spec=pltpu.PrefetchScalarGridSpec(num_scalar_...]
    dot_general x56 -> x0, matrix products: 58.2 us -> none  [the longest x28 29.2 us: transform(): jnp.dot(tables[0], jnp.concatenate([wave[0], wave[1]], 1), precision=HIGH...]
    sub x49 -> x2, other arithmetic: 39.6 us -> 8.12 us  [body(): slab_imag[s] - grads[s][1] / (lights[s] + 1.0)]
    dynamic_slice x6 -> x0, local copies, waits for them, and re-layouts: 18.4 us -> none  [the longest x4 17 us: add_window(): region = lax.dynamic_slice(totals, start, piece.shape)]
    another operation x1 -> x0, loops' own time: 18.1 us -> none  [body(): totals = lax.fori_loop(0, own_count, own_step, totals)]
  transfers between devices with their start and end apart: 8 -> 44, of which waited for: 5 -> 17; matrix products, arithmetic and copies ran while one was open for 4% -> 15% of each run, Pallas kernels for 0% -> 14%
where the time goes in v1:
time: 446 us; the launch traced here: 438 us
  starting transfers between devices  145 us (33%)
  waiting for transfers between devices  142 us (32%)
  Pallas kernels  60.8 us (14%)
  other arithmetic  60.3 us (14%)
  local copies, waits for them, and re-layouts  27.8 us (6%)
    ppermute x44, starting transfers between devices, shifted(): lax.ppermute(value, axis, [(source, source + steps) for source in range(f...  145 us
    ppermute x44, waiting for transfers between devices, shifted(): lax.ppermute(value, axis, [(source, source + steps) for source in range(f...  142 us
    pallas_call x7, Pallas kernels, call(): pl.pallas_call(kernel, grid_spec=pltpu.PrefetchScalarGridSpec(num_scalar_...  60.8 us
    concatenate x4, other arithmetic, halo(): return jnp.concatenate([above, tile, below], 1)  15.2 us
    slice x7, local copies, waits for them, and re-layouts, fold(): from_prev = shifted(totals[:, -width:], 'row', 1)  14.7 us
  transfers between devices with their start and end apart: 44, of which 17 were waited for; matrix products, arithmetic and copies ran while one was open for 15% of the time, Pallas kernels for 14%

profile of v1, /device:TPU:19, one launch (start us, length us, event | category | flops | bytes accessed | tf_op | source)
XLA Modules:
  0.0 438.5 jit_solution(4392502426992919819)
XLA Ops:
  0.6 7.1 %fusion.1 = (f32[4,512,512]{2,1,0:T(8,128)S(1)}, f32[4,512,512]{2,1,0:T(8,128)S(1)}) fusion(f32[4,512,512]{2,1,0:T(8,128)} %param.10, f32[4,512,512]{2,1,0:T(8,128)} %param.11), kind=kLoop, calls=%fused_computation.8 | loop fusion | flops 36700160 | bytes 16777216 | tf_op jit(solution)/shard_map/mul | solution.py:277
  11.2 3.2 collective-permute-start
  17.4 4.1 collective-permute-start.8
  21.6 2.2 collective-permute-start.4
  23.8 3.0 collective-permute-start.5
  26.9 21.5 %collective-permute-done = f32[2,512,128]{2,1,0:T(8,128)S(1)} collective-permute-done((f32[2,512,128]{2,1,0:T(8,128)S(1)}, f32[2,512,128]{2,1,0:T(8,128)S(1)}, u32[]{:S(2)}, u32[]{:S(2)}) %collective-permute-start) | collective-permute-done | bytes 524320 | tf_op jit(solution)/shard_map/ppermute | solution.py:22
  50.3 9.3 %collective-permute-done.1 = f32[2,512,128]{2,1,0:T(8,128)S(1)} collective-permute-done((f32[2,512,128]{2,1,0:T(8,128)S(1)}, f32[2,512,128]{2,1,0:T(8,128)S(1)}, u32[]{:S(2)}, u32[]{:S(2)}) %collective-permute-start.1) | collective-permute-done | bytes 524320 | tf_op jit(solution)/shard_map/ppermute | solution.py:22
  61.0 3.6 collective-permute-start.2
  64.6 6.2 %collective-permute-done.8 = f32[2,512,128]{2,1,0:T(8,128)S(1)} collective-permute-done((f32[2,512,128]{2,1,0:T(8,128)S(1)}, f32[2,512,128]{2,1,0:T(8,128)S(1)}, u32[]{:S(2)}, u32[]{:S(2)}) %collective-permute-start.8) | collective-permute-done | bytes 524320 | tf_op jit(solution)/shard_map/ppermute | solution.py:22
  70.8 4.6 %collective-permute-start.3 = (f32[2,128,768]{2,1,0:T(8,128)}, f32[2,128,768]{2,1,0:T(8,128)}, u32[]{:S(2)}, u32[]{:S(2)}) collective-permute-start(f32[2,128,768]{2,1,0:T(8,128)} %get-tuple-element.65), channel_id=1, source_target_pairs={{8,0},{16,8},{24,16},{9,1},{17,9},{25,17},{10,2},{18,10},{26,18},{... | collective-permute-start | bytes 2359304 | tf_op jit(solution)/shard_map/ppermute | solution.py:22
  76.5 5.6 %collective-permute-done.4 = f32[2,512,128]{2,1,0:T(8,128)S(1)} collective-permute-done((f32[2,512,128]{2,1,0:T(8,128)S(1)}, f32[2,512,128]{2,1,0:T(8,128)S(1)}, u32[]{:S(2)}, u32[]{:S(2)}) %collective-permute-start.4) | collective-permute-done | bytes 524320 | tf_op jit(solution)/shard_map/ppermute | solution.py:22
  84.0 3.4 collective-permute-start.13
  88.2 2.8 pad_maximum_fusion.17
  91.0 5.4 %collective-permute-start.6 = (f32[2,128,768]{2,1,0:T(8,128)}, f32[2,128,768]{2,1,0:T(8,128)}, u32[]{:S(2)}, u32[]{:S(2)}) collective-permute-start(f32[2,128,768]{2,1,0:T(8,128)} %get-tuple-element.66), channel_id=1, source_target_pairs={{0,8},{8,16},{16,24},{1,9},{9,17},{17,25},{2,10},{10,18},{18,26},{... | collective-permute-start | bytes 2359304 | tf_op jit(solution)/shard_map/ppermute | solution.py:22
  96.5 2.2 pad_maximum_fusion.13
  98.7 8.7 %collective-permute-done.12 = f32[2,512,128]{2,1,0:T(8,128)} collective-permute-done((f32[2,512,128]{2,1,0:T(8,128)}, f32[2,512,128]{2,1,0:T(8,128)}, u32[]{:S(2)}, u32[]{:S(2)}) %collective-permute-start.12) | collective-permute-done | bytes 524320 | tf_op jit(solution)/shard_map/ppermute | solution.py:22
  107.4 4.4 collective-permute-start.7
  111.8 3.0 collective-permute-start.10
  116.9 2.2 collective-permute-start.11
  119.1 3.5 collective-permute-start.14
  122.7 3.7 pad_maximum_fusion.padded_ref
  126.5 8.9 %shard_map.113 = (f32[4,2,256,256]{3,2,1,0:T(8,128)}, f32[4,2,256,256]{3,2,1,0:T(8,128)}, f32[1,768,768]{2,1,0:T(8,128)}) custom-call(s32[4,2]{1,0:T(4,128)S(1)} %copy.18.offset_ref, s32[1]{0:T(128)} %bitcast.4.count_ref, f32[2,768,768]{2,1,0:T(8,128)} %pad_maximum_fusion.padded_ref, f32[1,2,256,256]{3,2,1,0:T(8,128)S(1)} %bitcast.11, ...), custom_call_target="tpu_custom_call" | custom-call | flops 3221225472 | bytes 18612224 | tf_op jit(solution)/shard_map/pallas_call | solution.py:261
  137.2 2.4 collective-permute-start.15
  139.7 3.3 collective-permute-start.20
  143.0 3.7 pad_maximum_fusion.1.padded_ref
  146.7 8.9 %shard_map.114 = (f32[4,2,256,256]{3,2,1,0:T(8,128)}, f32[4,2,256,256]{3,2,1,0:T(8,128)}, f32[1,768,768]{2,1,0:T(8,128)}) custom-call(s32[4,2]{1,0:T(4,128)S(1)} %copy.18.offset_ref, s32[1]{0:T(128)} %bitcast.5.count_ref, f32[2,768,768]{2,1,0:T(8,128)} %pad_maximum_fusion.1.padded_ref, f32[4,2,256,256]{3,2,1,0:T(8,128)} %get-tuple-element.16.wave_ref, ...), custom_call_target="tpu_custom_call" | custom-call | flops 3221225472 | bytes 20185088 | tf_op jit(solution)/shard_map/pallas_call | solution.py:261
  157.7 3.2 collective-permute-start.21
  160.9 2.6 collective-permute-start.28
  163.4 3.9 pad_maximum_fusion.2.padded_ref
  167.3 8.9 %shard_map.115 = (f32[4,2,256,256]{3,2,1,0:T(8,128)}, f32[4,2,256,256]{3,2,1,0:T(8,128)}, f32[1,768,768]{2,1,0:T(8,128)}) custom-call(s32[4,2]{1,0:T(4,128)S(1)} %copy.18.offset_ref, s32[1]{0:T(128)} %bitcast.6.count_ref, f32[2,768,768]{2,1,0:T(8,128)} %pad_maximum_fusion.2.padded_ref, f32[4,2,256,256]{3,2,1,0:T(8,128)} %get-tuple-element.18.wave_ref, ...), custom_call_target="tpu_custom_call" | custom-call | flops 3221225472 | bytes 20185088 | tf_op jit(solution)/shard_map/pallas_call | solution.py:261
  178.3 3.8 collective-permute-start.29
  184.1 3.9 pad_maximum_fusion.3.padded_ref
  188.0 13.1 %shard_map.116 = (f32[4,2,256,256]{3,2,1,0:T(8,128)}, f32[3,768,768]{2,1,0:T(8,128)}) custom-call(s32[4,2]{1,0:T(4,128)S(1)} %copy.18.offset_ref, s32[1]{0:T(128)} %bitcast.7.count_ref, f32[2,768,768]{2,1,0:T(8,128)} %pad_maximum_fusion.3.padded_ref, f32[4,2,256,256]{3,2,1,0:T(8,128)} %get-tuple-element.20.wave_ref, f32[4,256,256]{2,1,0:T(8,128)S(1)} %bitcast.13, ...), custom_call_target="tpu_custom_call" | custom-call | flops 6442450944 | bytes 24379392 | tf_op jit(solution)/shard_map/pallas_call | solution.py:261
  201.2 8.8 %shard_map.117 = (f32[4,2,256,256]{3,2,1,0:T(8,128)}, f32[2,768,768]{2,1,0:T(8,128)}) custom-call(s32[4,2]{1,0:T(4,128)S(1)} %copy.18.offset_ref, s32[1]{0:T(128)} %bitcast.8.count_ref, f32[4,2,256,256]{3,2,1,0:T(8,128)} %get-tuple-element.18.wave_ref, f32[4,2,256,256]{3,2,1,0:T(8,128)} %get-tuple-element.19.window_ref, ...), custom_call_target="tpu_custom_call" | custom-call | flops 3221225472 | bytes 19922944 | tf_op jit(solution)/shard_map/pallas_call | solution.py:261
  209.9 8.6 %shard_map.118 = (f32[4,2,256,256]{3,2,1,0:T(8,128)}, f32[2,768,768]{2,1,0:T(8,128)}) custom-call(s32[4,2]{1,0:T(4,128)S(1)} %copy.18.offset_ref, s32[1]{0:T(128)} %bitcast.9.count_ref, f32[4,2,256,256]{3,2,1,0:T(8,128)} %get-tuple-element.16.wave_ref, f32[4,2,256,256]{3,2,1,0:T(8,128)} %get-tuple-element.17.window_ref, ...), custom_call_target="tpu_custom_call" | custom-call | flops 3221225472 | bytes 19922944 | tf_op jit(solution)/shard_map/pallas_call | solution.py:261
  218.6 2.7 fusion.28
  222.8 2.7 fusion.29
  225.6 3.6 shard_map.119
  230.9 9.0 %collective-permute-start.37 = (f32[1,128,768]{2,1,0:T(8,128)}, f32[1,128,768]{2,1,0:T(8,128)S(1)}, u32[]{:S(2)}, u32[]{:S(2)}) collective-permute-start(f32[1,128,768]{2,1,0:T(8,128)} %get-tuple-element.77), channel_id=1, source_target_pairs={{8,0},{16,8},{24,16},{9,1},{17,9},{25,17},{10,2},{18,10},{26,18},{... | collective-permute-start | bytes 1179656 | tf_op jit(solution)/shard_map/ppermute | solution.py:22
  240.6 2.2 collective-permute-start.24
  244.2 2.6 collective-permute-start.25
  246.8 3.3 collective-permute-start.32
  255.2 3.6 collective-permute-start.40
  258.8 2.3 pad_add_fusion.3
  265.0 2.7 collective-permute-start.17
  271.1 5.1 %collective-permute-start.26 = (f32[2,512,128]{2,1,0:T(8,128)}, f32[2,512,128]{2,1,0:T(8,128)S(1)}, u32[]{:S(2)}, u32[]{:S(2)}) collective-permute-start(f32[2,512,128]{2,1,0:T(8,128)} %get-tuple-element.60), channel_id=1, source_target_pairs={{0,1},{1,2},{2,3},{3,4},{4,5},{5,6},{6,7},{8,9},{9,10},{10,11},{11... | collective-permute-start | bytes 1572872 | tf_op jit(solution)/shard_map/ppermute | solution.py:22
  277.6 3.7 collective-permute-done.16
  281.4 20.1 %collective-permute-start.27 = (f32[2,512,128]{2,1,0:T(8,128)}, f32[2,512,128]{2,1,0:T(8,128)}, u32[]{:S(2)}, u32[]{:S(2)}) collective-permute-start(f32[2,512,128]{2,1,0:T(8,128)} %get-tuple-element.61), channel_id=1, source_target_pairs={{1,0},{2,1},{3,2},{4,3},{5,4},{6,5},{7,6},{9,8},{10,9},{11,10},{12... | collective-permute-start | bytes 1572872 | tf_op jit(solution)/shard_map/ppermute | solution.py:22
  304.8 3.4 collective-permute-start.35
  309.2 2.8 collective-permute-start.18
  314.3 12.4 %collective-permute-done.26 = f32[2,512,128]{2,1,0:T(8,128)S(1)} collective-permute-done((f32[2,512,128]{2,1,0:T(8,128)}, f32[2,512,128]{2,1,0:T(8,128)S(1)}, u32[]{:S(2)}, u32[]{:S(2)}) %collective-permute-start.26) | collective-permute-done | bytes 524320 | tf_op jit(solution)/shard_map/ppermute | solution.py:22
  328.6 8.9 %collective-permute-done.27 = f32[2,512,128]{2,1,0:T(8,128)} collective-permute-done((f32[2,512,128]{2,1,0:T(8,128)}, f32[2,512,128]{2,1,0:T(8,128)}, u32[]{:S(2)}, u32[]{:S(2)}) %collective-permute-start.27) | collective-permute-done | bytes 524320 | tf_op jit(solution)/shard_map/ppermute | solution.py:22
  339.4 9.9 %collective-permute-done.34 = f32[2,512,128]{2,1,0:T(8,128)S(1)} collective-permute-done((f32[2,512,128]{2,1,0:T(8,128)}, f32[2,512,128]{2,1,0:T(8,128)S(1)}, u32[]{:S(2)}, u32[]{:S(2)}) %collective-permute-start.34) | collective-permute-done | bytes 524320 | tf_op jit(solution)/shard_map/ppermute | solution.py:22
  352.5 13.1 %collective-permute-done.35 = f32[2,512,128]{2,1,0:T(8,128)} collective-permute-done((f32[2,512,128]{2,1,0:T(8,128)}, f32[2,512,128]{2,1,0:T(8,128)}, u32[]{:S(2)}, u32[]{:S(2)}) %collective-permute-start.35) | collective-permute-done | bytes 524320 | tf_op jit(solution)/shard_map/ppermute | solution.py:22
  369.0 8.3 %collective-permute-done.18 = f32[2,512,128]{2,1,0:T(8,128)} collective-permute-done((f32[2,512,128]{2,1,0:T(8,128)}, f32[2,512,128]{2,1,0:T(8,128)}, u32[]{:S(2)}, u32[]{:S(2)}) %collective-permute-start.18) | collective-permute-done | bytes 524320 | tf_op jit(solution)/shard_map/ppermute | solution.py:22
  379.2 3.3 collective-permute-done.19
  385.9 13.9 %collective-permute-done.42 = f32[3,512,128]{2,1,0:T(8,128)S(1)} collective-permute-done((f32[3,512,128]{2,1,0:T(8,128)S(1)}, f32[3,512,128]{2,1,0:T(8,128)S(1)}, u32[]{:S(2)}, u32[]{:S(2)}) %collective-permute-start.42) | collective-permute-done | bytes 786464 | tf_op jit(solution)/shard_map/ppermute | solution.py:22
  401.7 3.2 collective-permute-done.43
  407.2 3.8 collective-permute-done.22
  412.9 9.4 %collective-permute-done.30 = f32[1,512,128]{2,1,0:T(8,128)S(1)} collective-permute-done((f32[1,512,128]{2,1,0:T(8,128)}, f32[1,512,128]{2,1,0:T(8,128)S(1)}, u32[]{:S(2)}, u32[]{:S(2)}) %collective-permute-start.30) | collective-permute-done | bytes 262176 | tf_op jit(solution)/shard_map/ppermute | solution.py:22
  423.0 3.8 fusion.15
  427.3 4.3 fusion.13
  431.7 4.3 pad_maximum_fusion.5
  436.0 2.5 pad_maximum_fusion.4
  (205 shorter events, 71.7 us)
Async XLA Ops:
  11.1 48.5 %copy-start.18 = (f32[1,512,512]{2,1,0:T(8,128)}, f32[1,512,512]{2,1,0:T(8,128)S(1)}, u32[]{:S(2)}) copy-start(f32[1,512,512]{2,1,0:T(8,128)S(1)} %get-tuple-element.50) | copy-start | bytes 3145732
  11.1 48.5 %copy-start.20 = (f32[1,512,512]{2,1,0:T(8,128)}, f32[1,512,512]{2,1,0:T(8,128)S(1)}, u32[]{:S(2)}) copy-start(f32[1,512,512]{2,1,0:T(8,128)S(1)} %get-tuple-element.95) | copy-start | bytes 3145732
  11.2 37.2 %collective-permute-start = (f32[2,512,128]{2,1,0:T(8,128)S(1)}, f32[2,512,128]{2,1,0:T(8,128)S(1)}, u32[]{:S(2)}, u32[]{:S(2)}) collective-permute-start(f32[2,512,128]{2,1,0:T(8,128)S(1)} %get-tuple-element.78), channel_id=1, source_target_pairs={{0,1},{1,2},{2,3},{3,4},{4,5},{5,6},{6,7},{8,9},{9,10},{10,11},{11... | collective-permute-start | bytes 1572872 | tf_op jit(solution)/shard_map/ppermute | solution.py:22
  14.4 45.2 %collective-permute-start.1 = (f32[2,512,128]{2,1,0:T(8,128)S(1)}, f32[2,512,128]{2,1,0:T(8,128)S(1)}, u32[]{:S(2)}, u32[]{:S(2)}) collective-permute-start(f32[2,512,128]{2,1,0:T(8,128)S(1)} %get-tuple-element.79), channel_id=1, source_target_pairs={{1,0},{2,1},{3,2},{4,3},{5,4},{6,5},{7,6},{9,8},{10,9},{11,10},{12... | collective-permute-start | bytes 1572872 | tf_op jit(solution)/shard_map/ppermute | solution.py:22
  17.4 53.5 %collective-permute-start.8 = (f32[2,512,128]{2,1,0:T(8,128)S(1)}, f32[2,512,128]{2,1,0:T(8,128)S(1)}, u32[]{:S(2)}, u32[]{:S(2)}) collective-permute-start(f32[2,512,128]{2,1,0:T(8,128)S(1)} %get-tuple-element.82), channel_id=1, source_target_pairs={{0,1},{1,2},{2,3},{3,4},{4,5},{5,6},{6,7},{8,9},{9,10},{10,11},{11... | collective-permute-start | bytes 1572872 | tf_op jit(solution)/shard_map/ppermute | solution.py:22
  21.5 66.5 %copy-start.54 = (s32[1,1,4,2]{2,3,1,0:T(2,128)S(1)}, s32[1,1,4,2]{2,3,1,0:T(2,128)}, u32[]{:S(2)}) copy-start(s32[1,1,4,2]{2,3,1,0:T(2,128)} %param.14) | copy-start | bytes 100
  21.6 60.5 %collective-permute-start.4 = (f32[2,512,128]{2,1,0:T(8,128)S(1)}, f32[2,512,128]{2,1,0:T(8,128)S(1)}, u32[]{:S(2)}, u32[]{:S(2)}) collective-permute-start(f32[2,512,128]{2,1,0:T(8,128)S(1)} %get-tuple-element.80), channel_id=1, source_target_pairs={{0,1},{1,2},{2,3},{3,4},{4,5},{5,6},{6,7},{8,9},{9,10},{10,11},{11... | collective-permute-start | bytes 1572872 | tf_op jit(solution)/shard_map/ppermute | solution.py:22
  23.8 60.2 %collective-permute-start.5 = (f32[2,512,128]{2,1,0:T(8,128)S(1)}, f32[2,512,128]{2,1,0:T(8,128)S(1)}, u32[]{:S(2)}, u32[]{:S(2)}) collective-permute-start(f32[2,512,128]{2,1,0:T(8,128)S(1)} %get-tuple-element.81), channel_id=1, source_target_pairs={{1,0},{2,1},{3,2},{4,3},{5,4},{6,5},{7,6},{9,8},{10,9},{11,10},{12... | collective-permute-start | bytes 1572872 | tf_op jit(solution)/shard_map/ppermute | solution.py:22
  48.4 39.7 %copy-start.37 = (f32[2,512,128]{2,1,0:T(8,128)}, f32[2,512,128]{2,1,0:T(8,128)S(1)}, u32[]{:S(2)}) copy-start(f32[2,512,128]{2,1,0:T(8,128)S(1)} %collective-permute-done) | copy-start | bytes 1572868
  48.4 42.7 %collective-permute-start.9 = (f32[2,512,128]{2,1,0:T(8,128)}, f32[2,512,128]{2,1,0:T(8,128)}, u32[]{:S(2)}, u32[]{:S(2)}) collective-permute-start(f32[2,512,128]{2,1,0:T(8,128)} %get-tuple-element.83), channel_id=1, source_target_pairs={{1,0},{2,1},{3,2},{4,3},{5,4},{6,5},{7,6},{9,8},{10,9},{11,10},{12... | collective-permute-start | bytes 1572872 | tf_op jit(solution)/shard_map/ppermute | solution.py:22
  59.6 28.4 %copy-start.39 = (f32[2,512,128]{2,1,0:T(8,128)}, f32[2,512,128]{2,1,0:T(8,128)S(1)}, u32[]{:S(2)}) copy-start(f32[2,512,128]{2,1,0:T(8,128)S(1)} %collective-permute-done.1) | copy-start | bytes 1572868
  61.0 55.9 %collective-permute-start.2 = (f32[2,128,768]{2,1,0:T(8,128)}, f32[2,128,768]{2,1,0:T(8,128)}, u32[]{:S(2)}, u32[]{:S(2)}) collective-permute-start(f32[2,128,768]{2,1,0:T(8,128)} %get-tuple-element.64), channel_id=1, source_target_pairs={{0,8},{8,16},{16,24},{1,9},{9,17},{17,25},{2,10},{10,18},{18,26},{... | collective-permute-start | bytes 2359304 | tf_op jit(solution)/shard_map/ppermute | solution.py:22
  70.8 48.3 %collective-permute-start.3 = (f32[2,128,768]{2,1,0:T(8,128)}, f32[2,128,768]{2,1,0:T(8,128)}, u32[]{:S(2)}, u32[]{:S(2)}) collective-permute-start(f32[2,128,768]{2,1,0:T(8,128)} %get-tuple-element.65), channel_id=1, source_target_pairs={{8,0},{16,8},{24,16},{9,1},{17,9},{25,17},{10,2},{18,10},{26,18},{... | collective-permute-start | bytes 2359304 | tf_op jit(solution)/shard_map/ppermute | solution.py:22
  82.1 25.3 %collective-permute-start.12 = (f32[2,512,128]{2,1,0:T(8,128)}, f32[2,512,128]{2,1,0:T(8,128)}, u32[]{:S(2)}, u32[]{:S(2)}) collective-permute-start(f32[2,512,128]{2,1,0:T(8,128)} %get-tuple-element.84), channel_id=1, source_target_pairs={{0,1},{1,2},{2,3},{3,4},{4,5},{5,6},{6,7},{8,9},{9,10},{10,11},{11... | collective-permute-start | bytes 1572872 | tf_op jit(solution)/shard_map/ppermute | solution.py:22
  84.0 27.7 %collective-permute-start.13 = (f32[2,512,128]{2,1,0:T(8,128)}, f32[2,512,128]{2,1,0:T(8,128)}, u32[]{:S(2)}, u32[]{:S(2)}) collective-permute-start(f32[2,512,128]{2,1,0:T(8,128)} %get-tuple-element.85), channel_id=1, source_target_pairs={{1,0},{2,1},{3,2},{4,3},{5,4},{6,5},{7,6},{9,8},{10,9},{11,10},{12... | collective-permute-start | bytes 1572872 | tf_op jit(solution)/shard_map/ppermute | solution.py:22
  91.0 31.6 %copy-start.19 = (f32[1,512,512]{2,1,0:T(8,128)S(1)}, f32[1,512,512]{2,1,0:T(8,128)}, u32[]{:S(2)}) copy-start(f32[1,512,512]{2,1,0:T(8,128)} %copy-done.18) | copy-start | bytes 3145732
  91.0 31.6 %copy-start.21 = (f32[1,512,512]{2,1,0:T(8,128)S(1)}, f32[1,512,512]{2,1,0:T(8,128)}, u32[]{:S(2)}) copy-start(f32[1,512,512]{2,1,0:T(8,128)} %copy-done.20) | copy-start | bytes 3145732
  91.0 31.6 %copy-start.38 = (f32[2,512,128]{2,1,0:T(8,128)S(1)}, f32[2,512,128]{2,1,0:T(8,128)}, u32[]{:S(2)}) copy-start(f32[2,512,128]{2,1,0:T(8,128)} %copy-done.37) | copy-start | bytes 1572868
  91.0 31.6 %copy-start.40 = (f32[2,512,128]{2,1,0:T(8,128)S(1)}, f32[2,512,128]{2,1,0:T(8,128)}, u32[]{:S(2)}) copy-start(f32[2,512,128]{2,1,0:T(8,128)} %copy-done.39) | copy-start | bytes 1572868
  91.0 46.2 %collective-permute-start.6 = (f32[2,128,768]{2,1,0:T(8,128)}, f32[2,128,768]{2,1,0:T(8,128)}, u32[]{:S(2)}, u32[]{:S(2)}) collective-permute-start(f32[2,128,768]{2,1,0:T(8,128)} %get-tuple-element.66), channel_id=1, source_target_pairs={{0,8},{8,16},{16,24},{1,9},{9,17},{17,25},{2,10},{10,18},{18,26},{... | collective-permute-start | bytes 2359304 | tf_op jit(solution)/shard_map/ppermute | solution.py:22
  107.4 32.3 %collective-permute-start.7 = (f32[2,128,768]{2,1,0:T(8,128)}, f32[2,128,768]{2,1,0:T(8,128)}, u32[]{:S(2)}, u32[]{:S(2)}) collective-permute-start(f32[2,128,768]{2,1,0:T(8,128)} %get-tuple-element.67), channel_id=1, source_target_pairs={{8,0},{16,8},{24,16},{9,1},{17,9},{25,17},{10,2},{18,10},{26,18},{... | collective-permute-start | bytes 2359304 | tf_op jit(solution)/shard_map/ppermute | solution.py:22
  111.8 45.9 %collective-permute-start.10 = (f32[2,128,768]{2,1,0:T(8,128)}, f32[2,128,768]{2,1,0:T(8,128)}, u32[]{:S(2)}, u32[]{:S(2)}) collective-permute-start(f32[2,128,768]{2,1,0:T(8,128)} %get-tuple-element.68), channel_id=1, source_target_pairs={{0,8},{8,16},{16,24},{1,9},{9,17},{17,25},{2,10},{10,18},{18,26},{... | collective-permute-start | bytes 2359304 | tf_op jit(solution)/shard_map/ppermute | solution.py:22
  116.9 43.9 %collective-permute-start.11 = (f32[2,128,768]{2,1,0:T(8,128)}, f32[2,128,768]{2,1,0:T(8,128)}, u32[]{:S(2)}, u32[]{:S(2)}) collective-permute-start(f32[2,128,768]{2,1,0:T(8,128)} %get-tuple-element.69), channel_id=1, source_target_pairs={{8,0},{16,8},{24,16},{9,1},{17,9},{25,17},{10,2},{18,10},{26,18},{... | collective-permute-start | bytes 2359304 | tf_op jit(solution)/shard_map/ppermute | solution.py:22
  119.1 59.1 %collective-permute-start.14 = (f32[2,128,768]{2,1,0:T(8,128)}, f32[2,128,768]{2,1,0:T(8,128)S(1)}, u32[]{:S(2)}, u32[]{:S(2)}) collective-permute-start(f32[2,128,768]{2,1,0:T(8,128)} %get-tuple-element.70), channel_id=1, source_target_pairs={{0,8},{8,16},{16,24},{1,9},{9,17},{17,25},{2,10},{10,18},{18,26},{... | collective-permute-start | bytes 2359304 | tf_op jit(solution)/shard_map/ppermute | solution.py:22
  137.2 44.8 %collective-permute-start.15 = (f32[2,128,768]{2,1,0:T(8,128)S(1)}, f32[2,128,768]{2,1,0:T(8,128)}, u32[]{:S(2)}, u32[]{:S(2)}) collective-permute-start(f32[2,128,768]{2,1,0:T(8,128)S(1)} %get-tuple-element.71), channel_id=1, source_target_pairs={{8,0},{16,8},{24,16},{9,1},{17,9},{25,17},{10,2},{18,10},{26,18},{... | collective-permute-start | bytes 2359304 | tf_op jit(solution)/shard_map/ppermute | solution.py:22
  139.7 91.2 %collective-permute-start.20 = (f32[1,128,768]{2,1,0:T(8,128)}, f32[1,128,768]{2,1,0:T(8,128)}, u32[]{:S(2)}, u32[]{:S(2)}) collective-permute-start(f32[1,128,768]{2,1,0:T(8,128)} %get-tuple-element.72), channel_id=1, source_target_pairs={{0,8},{8,16},{16,24},{1,9},{9,17},{17,25},{2,10},{10,18},{18,26},{... | collective-permute-start | bytes 1179656 | tf_op jit(solution)/shard_map/ppermute | solution.py:22
  157.7 82.2 %collective-permute-start.21 = (f32[1,128,768]{2,1,0:T(8,128)S(1)}, f32[1,128,768]{2,1,0:T(8,128)S(1)}, u32[]{:S(2)}, u32[]{:S(2)}) collective-permute-start(f32[1,128,768]{2,1,0:T(8,128)S(1)} %get-tuple-element.73), channel_id=1, source_target_pairs={{8,0},{16,8},{24,16},{9,1},{17,9},{25,17},{10,2},{18,10},{26,18},{... | collective-permute-start | bytes 1179656 | tf_op jit(solution)/shard_map/ppermute | solution.py:22
  160.9 83.3 %collective-permute-start.28 = (f32[1,128,768]{2,1,0:T(8,128)}, f32[1,128,768]{2,1,0:T(8,128)}, u32[]{:S(2)}, u32[]{:S(2)}) collective-permute-start(f32[1,128,768]{2,1,0:T(8,128)} %get-tuple-element.74), channel_id=1, source_target_pairs={{0,8},{8,16},{16,24},{1,9},{9,17},{17,25},{2,10},{10,18},{18,26},{... | collective-permute-start | bytes 1179656 | tf_op jit(solution)/shard_map/ppermute | solution.py:22
  178.3 68.6 %collective-permute-start.29 = (f32[1,128,768]{2,1,0:T(8,128)}, f32[1,128,768]{2,1,0:T(8,128)}, u32[]{:S(2)}, u32[]{:S(2)}) collective-permute-start(f32[1,128,768]{2,1,0:T(8,128)} %get-tuple-element.75), channel_id=1, source_target_pairs={{8,0},{16,8},{24,16},{9,1},{17,9},{25,17},{10,2},{18,10},{26,18},{... | collective-permute-start | bytes 1179656 | tf_op jit(solution)/shard_map/ppermute | solution.py:22
  182.1 71.2 %collective-permute-start.36 = (f32[1,128,768]{2,1,0:T(8,128)}, f32[1,128,768]{2,1,0:T(8,128)}, u32[]{:S(2)}, u32[]{:S(2)}) collective-permute-start(f32[1,128,768]{2,1,0:T(8,128)} %get-tuple-element.76), channel_id=1, source_target_pairs={{0,8},{8,16},{16,24},{1,9},{9,17},{17,25},{2,10},{10,18},{18,26},{... | collective-permute-start | bytes 1179656 | tf_op jit(solution)/shard_map/ppermute | solution.py:22
  201.2 20.1 %slice-start.2 = ((s8[7077888]{0:T(1024)(128)(4,1)}), s8[4194304]{0:T(1024)(128)(4,1)S(1)}, s32[]{:S(2)}) async-start(s8[7077888]{0:T(1024)(128)(4,1)} %bitcast.16), calls=%async_computation.2 | async-start | bytes 8388608
  229.2 21.0 %copy-start.29 = (f32[1,768,768]{2,1,0:T(8,128)S(1)}, f32[1,768,768]{2,1,0:T(8,128)}, u32[]{:S(2)}) copy-start(f32[1,768,768]{2,1,0:T(8,128)} %get-tuple-element.26) | copy-start | bytes 7077892
  230.9 24.3 %collective-permute-start.37 = (f32[1,128,768]{2,1,0:T(8,128)}, f32[1,128,768]{2,1,0:T(8,128)S(1)}, u32[]{:S(2)}, u32[]{:S(2)}) collective-permute-start(f32[1,128,768]{2,1,0:T(8,128)} %get-tuple-element.77), channel_id=1, source_target_pairs={{8,0},{16,8},{24,16},{9,1},{17,9},{25,17},{10,2},{18,10},{26,18},{... | collective-permute-start | bytes 1179656 | tf_op jit(solution)/shard_map/ppermute | solution.py:22
  240.6 18.2 %copy-start.30 = (f32[1,768,768]{2,1,0:T(8,128)S(1)}, f32[1,768,768]{2,1,0:T(8,128)}, u32[]{:S(2)}) copy-start(f32[1,768,768]{2,1,0:T(8,128)} %get-tuple-element.28) | copy-start | bytes 7077892
  240.6 22.4 %collective-permute-start.24 = (f32[2,128,768]{2,1,0:T(8,128)}, f32[2,128,768]{2,1,0:T(8,128)S(1)}, u32[]{:S(2)}, u32[]{:S(2)}) collective-permute-start(f32[2,128,768]{2,1,0:T(8,128)} %get-tuple-element.36), channel_id=1, source_target_pairs={{0,8},{8,16},{16,24},{1,9},{9,17},{17,25},{2,10},{10,18},{18,26},{... | collective-permute-start | bytes 2359304 | tf_op jit(solution)/shard_map/ppermute | solution.py:22
  242.8 24.9 %slice-start.6 = ((s8[4718592]{0:T(1024)(128)(4,1)}), s8[4194304]{0:T(1024)(128)(4,1)S(1)}, s32[]{:S(2)}) async-start(s8[4718592]{0:T(1024)(128)(4,1)} %bitcast.20), calls=%async_computation.6 | async-start | bytes 8388608
  244.2 20.7 %collective-permute-start.25 = (f32[2,128,768]{2,1,0:T(8,128)S(1)}, f32[2,128,768]{2,1,0:T(8,128)S(1)}, u32[]{:S(2)}, u32[]{:S(2)}) collective-permute-start(f32[2,128,768]{2,1,0:T(8,128)S(1)} %copy-done.50), channel_id=1, source_target_pairs={{8,0},{16,8},{24,16},{9,1},{17,9},{25,17},{10,2},{18,10},{26,18},{... | collective-permute-start | bytes 2359304 | tf_op jit(solution)/shard_map/ppermute | solution.py:22
  246.8 20.9 %slice-start.7 = ((s8[4718592]{0:T(1024)(128)(4,1)}), s8[524288]{0:T(1024)(128)(4,1)S(1)}, s32[]{:S(2)}) async-start(s8[4718592]{0:T(1024)(128)(4,1)} %bitcast.20), calls=%async_computation.7 | async-start | bytes 1048576
  246.8 22.3 %collective-permute-start.32 = (f32[2,128,768]{2,1,0:T(8,128)S(1)}, f32[2,128,768]{2,1,0:T(8,128)S(1)}, u32[]{:S(2)}, u32[]{:S(2)}) collective-permute-start(f32[2,128,768]{2,1,0:T(8,128)S(1)} %copy-done.49), channel_id=1, source_target_pairs={{0,8},{8,16},{16,24},{1,9},{9,17},{17,25},{2,10},{10,18},{18,26},{... | collective-permute-start | bytes 2359304 | tf_op jit(solution)/shard_map/ppermute | solution.py:22
  253.2 17.8 %collective-permute-start.33 = (f32[2,128,768]{2,1,0:T(8,128)S(1)}, f32[2,128,768]{2,1,0:T(8,128)S(1)}, u32[]{:S(2)}, u32[]{:S(2)}) collective-permute-start(f32[2,128,768]{2,1,0:T(8,128)S(1)} %copy-done.48), channel_id=1, source_target_pairs={{8,0},{16,8},{24,16},{9,1},{17,9},{25,17},{10,2},{18,10},{26,18},{... | collective-permute-start | bytes 2359304 | tf_op jit(solution)/shard_map/ppermute | solution.py:22
  255.2 49.7 %collective-permute-start.40 = (f32[3,128,768]{2,1,0:T(8,128)S(1)}, f32[3,128,768]{2,1,0:T(8,128)S(1)}, u32[]{:S(2)}, u32[]{:S(2)}) collective-permute-start(f32[3,128,768]{2,1,0:T(8,128)S(1)} %copy-done.44), channel_id=1, source_target_pairs={{0,8},{8,16},{16,24},{1,9},{9,17},{17,25},{2,10},{10,18},{18,26},{... | collective-permute-start | bytes 3538952 | tf_op jit(solution)/shard_map/ppermute | solution.py:22
  263.0 18.4 %collective-permute-start.16 = (f32[2,128,768]{2,1,0:T(8,128)S(1)}, f32[2,128,768]{2,1,0:T(8,128)S(1)}, u32[]{:S(2)}, u32[]{:S(2)}) collective-permute-start(f32[2,128,768]{2,1,0:T(8,128)S(1)} %get-tuple-element.34), channel_id=1, source_target_pairs={{0,8},{8,16},{16,24},{1,9},{9,17},{17,25},{2,10},{10,18},{18,26},{... | collective-permute-start | bytes 2359304 | tf_op jit(solution)/shard_map/ppermute | solution.py:22
  265.0 36.5 %collective-permute-start.17 = (f32[2,128,768]{2,1,0:T(8,128)S(1)}, f32[2,128,768]{2,1,0:T(8,128)S(1)}, u32[]{:S(2)}, u32[]{:S(2)}) collective-permute-start(f32[2,128,768]{2,1,0:T(8,128)S(1)} %get-tuple-element.35), channel_id=1, source_target_pairs={{8,0},{16,8},{24,16},{9,1},{17,9},{25,17},{10,2},{18,10},{26,18},{... | collective-permute-start | bytes 2359304 | tf_op jit(solution)/shard_map/ppermute | solution.py:22
  269.1 39.1 %collective-permute-start.41 = (f32[3,128,768]{2,1,0:T(8,128)S(1)}, f32[3,128,768]{2,1,0:T(8,128)S(1)}, u32[]{:S(2)}, u32[]{:S(2)}) collective-permute-start(f32[3,128,768]{2,1,0:T(8,128)S(1)} %copy-done.43), channel_id=1, source_target_pairs={{8,0},{16,8},{24,16},{9,1},{17,9},{25,17},{10,2},{18,10},{26,18},{... | collective-permute-start | bytes 3538952 | tf_op jit(solution)/shard_map/ppermute | solution.py:22
  271.1 32.3 %slice-start = ((s8[4718592]{0:T(1024)(128)(4,1)}), s8[4194304]{0:T(1024)(128)(4,1)S(1)}, s32[]{:S(2)}) async-start(s8[4718592]{0:T(1024)(128)(4,1)} %bitcast.14), calls=%async_computation | async-start | bytes 8388608
  271.1 32.3 %slice-start.1 = ((s8[4718592]{0:T(1024)(128)(4,1)}), s8[524288]{0:T(1024)(128)(4,1)S(1)}, s32[]{:S(2)}) async-start(s8[4718592]{0:T(1024)(128)(4,1)} %bitcast.14), calls=%async_computation.1 | async-start | bytes 1048576
  271.1 55.6 %collective-permute-start.26 = (f32[2,512,128]{2,1,0:T(8,128)}, f32[2,512,128]{2,1,0:T(8,128)S(1)}, u32[]{:S(2)}, u32[]{:S(2)}) collective-permute-start(f32[2,512,128]{2,1,0:T(8,128)} %get-tuple-element.60), channel_id=1, source_target_pairs={{0,1},{1,2},{2,3},{3,4},{4,5},{5,6},{6,7},{8,9},{9,10},{10,11},{11... | collective-permute-start | bytes 1572872 | tf_op jit(solution)/shard_map/ppermute | solution.py:22
  281.4 56.1 %collective-permute-start.27 = (f32[2,512,128]{2,1,0:T(8,128)}, f32[2,512,128]{2,1,0:T(8,128)}, u32[]{:S(2)}, u32[]{:S(2)}) collective-permute-start(f32[2,512,128]{2,1,0:T(8,128)} %get-tuple-element.61), channel_id=1, source_target_pairs={{1,0},{2,1},{3,2},{4,3},{5,4},{6,5},{7,6},{9,8},{10,9},{11,10},{12... | collective-permute-start | bytes 1572872 | tf_op jit(solution)/shard_map/ppermute | solution.py:22
  301.5 47.8 %collective-permute-start.34 = (f32[2,512,128]{2,1,0:T(8,128)}, f32[2,512,128]{2,1,0:T(8,128)S(1)}, u32[]{:S(2)}, u32[]{:S(2)}) collective-permute-start(f32[2,512,128]{2,1,0:T(8,128)} %get-tuple-element.62), channel_id=1, source_target_pairs={{0,1},{1,2},{2,3},{3,4},{4,5},{5,6},{6,7},{8,9},{9,10},{10,11},{11... | collective-permute-start | bytes 1572872 | tf_op jit(solution)/shard_map/ppermute | solution.py:22
  304.8 60.8 %collective-permute-start.35 = (f32[2,512,128]{2,1,0:T(8,128)}, f32[2,512,128]{2,1,0:T(8,128)}, u32[]{:S(2)}, u32[]{:S(2)}) collective-permute-start(f32[2,512,128]{2,1,0:T(8,128)} %get-tuple-element.63), channel_id=1, source_target_pairs={{1,0},{2,1},{3,2},{4,3},{5,4},{6,5},{7,6},{9,8},{10,9},{11,10},{12... | collective-permute-start | bytes 1572872 | tf_op jit(solution)/shard_map/ppermute | solution.py:22
  309.2 68.0 %collective-permute-start.18 = (f32[2,512,128]{2,1,0:T(8,128)}, f32[2,512,128]{2,1,0:T(8,128)}, u32[]{:S(2)}, u32[]{:S(2)}) collective-permute-start(f32[2,512,128]{2,1,0:T(8,128)} %get-tuple-element.58), channel_id=1, source_target_pairs={{0,1},{1,2},{2,3},{3,4},{4,5},{5,6},{6,7},{8,9},{9,10},{10,11},{11... | collective-permute-start | bytes 1572872 | tf_op jit(solution)/shard_map/ppermute | solution.py:22
  326.7 55.7 %collective-permute-start.19 = (f32[2,512,128]{2,1,0:T(8,128)}, f32[2,512,128]{2,1,0:T(8,128)S(1)}, u32[]{:S(2)}, u32[]{:S(2)}) collective-permute-start(f32[2,512,128]{2,1,0:T(8,128)} %get-tuple-element.59), channel_id=1, source_target_pairs={{1,0},{2,1},{3,2},{4,3},{5,4},{6,5},{7,6},{9,8},{10,9},{11,10},{12... | collective-permute-start | bytes 1572872 | tf_op jit(solution)/shard_map/ppermute | solution.py:22
  337.5 62.2 %collective-permute-start.42 = (f32[3,512,128]{2,1,0:T(8,128)S(1)}, f32[3,512,128]{2,1,0:T(8,128)S(1)}, u32[]{:S(2)}, u32[]{:S(2)}) collective-permute-start(f32[3,512,128]{2,1,0:T(8,128)S(1)} %get-tuple-element.40), channel_id=1, source_target_pairs={{0,1},{1,2},{2,3},{3,4},{4,5},{5,6},{6,7},{8,9},{9,10},{10,11},{11... | collective-permute-start | bytes 2359304 | tf_op jit(solution)/shard_map/ppermute | solution.py:22
  349.3 55.5 %collective-permute-start.43 = (f32[3,512,128]{2,1,0:T(8,128)S(1)}, f32[3,512,128]{2,1,0:T(8,128)S(1)}, u32[]{:S(2)}, u32[]{:S(2)}) collective-permute-start(f32[3,512,128]{2,1,0:T(8,128)S(1)} %get-tuple-element.41), channel_id=1, source_target_pairs={{1,0},{2,1},{3,2},{4,3},{5,4},{6,5},{7,6},{9,8},{10,9},{11,10},{12... | collective-permute-start | bytes 2359304 | tf_op jit(solution)/shard_map/ppermute | solution.py:22
  365.6 34.1 %copy-start.53 = (f32[1,512,128]{2,1,0:T(8,128)S(1)}, f32[1,512,128]{2,1,0:T(8,128)}, u32[]{:S(2)}) copy-start(f32[1,512,128]{2,1,0:T(8,128)} %get-tuple-element.89) | copy-start | bytes 786436
  365.6 45.4 %collective-permute-start.22 = (f32[1,512,128]{2,1,0:T(8,128)}, f32[1,512,128]{2,1,0:T(8,128)S(1)}, u32[]{:S(2)}, u32[]{:S(2)}) collective-permute-start(f32[1,512,128]{2,1,0:T(8,128)} %get-tuple-element.86), channel_id=1, source_target_pairs={{0,1},{1,2},{2,3},{3,4},{4,5},{5,6},{6,7},{8,9},{9,10},{10,11},{11... | collective-permute-start | bytes 786440 | tf_op jit(solution)/shard_map/ppermute | solution.py:22
  377.3 35.6 %collective-permute-start.23 = (f32[1,512,128]{2,1,0:T(8,128)}, f32[1,512,128]{2,1,0:T(8,128)S(1)}, u32[]{:S(2)}, u32[]{:S(2)}) collective-permute-start(f32[1,512,128]{2,1,0:T(8,128)} %get-tuple-element.87), channel_id=1, source_target_pairs={{1,0},{2,1},{3,2},{4,3},{5,4},{6,5},{7,6},{9,8},{10,9},{11,10},{12... | collective-permute-start | bytes 786440 | tf_op jit(solution)/shard_map/ppermute | solution.py:22
  382.4 39.9 %collective-permute-start.30 = (f32[1,512,128]{2,1,0:T(8,128)}, f32[1,512,128]{2,1,0:T(8,128)S(1)}, u32[]{:S(2)}, u32[]{:S(2)}) collective-permute-start(f32[1,512,128]{2,1,0:T(8,128)} %get-tuple-element.88), channel_id=1, source_target_pairs={{0,1},{1,2},{2,3},{3,4},{4,5},{5,6},{6,7},{8,9},{9,10},{10,11},{11... | collective-permute-start | bytes 786440 | tf_op jit(solution)/shard_map/ppermute | solution.py:22
  384.4 38.7 %copy-start.11 = (f32[4,512,512]{2,1,0:T(8,128)S(1)}, f32[4,512,512]{2,1,0:T(8,128)}, u32[]{:S(2)}) copy-start(f32[4,512,512]{2,1,0:T(8,128)} %copy-done.10) | copy-start | bytes 12582916
  385.9 37.2 %copy-start.9 = (f32[4,512,512]{2,1,0:T(8,128)S(1)}, f32[4,512,512]{2,1,0:T(8,128)}, u32[]{:S(2)}) copy-start(f32[4,512,512]{2,1,0:T(8,128)} %copy-done.8) | copy-start | bytes 12582916
  385.9 37.2 %copy-start.23 = (f32[1,512,768]{2,1,0:T(8,128)S(1)}, f32[1,512,768]{2,1,0:T(8,128)}, u32[]{:S(2)}) copy-start(f32[1,512,768]{2,1,0:T(8,128)} %copy-done.22) | copy-start | bytes 4718596
  399.7 23.3 %collective-permute-start.31 = (f32[1,512,128]{2,1,0:T(8,128)S(1)}, f32[1,512,128]{2,1,0:T(8,128)}, u32[]{:S(2)}, u32[]{:S(2)}) collective-permute-start(f32[1,512,128]{2,1,0:T(8,128)S(1)} %copy-done.53), channel_id=1, source_target_pairs={{1,0},{2,1},{3,2},{4,3},{5,4},{6,5},{7,6},{9,8},{10,9},{11,10},{12... | collective-permute-start | bytes 786440 | tf_op jit(solution)/shard_map/ppermute | solution.py:22
  404.8 22.0 %collective-permute-start.38 = (f32[1,512,128]{2,1,0:T(8,128)}, f32[1,512,128]{2,1,0:T(8,128)}, u32[]{:S(2)}, u32[]{:S(2)}) collective-permute-start(f32[1,512,128]{2,1,0:T(8,128)} %get-tuple-element.90), channel_id=1, source_target_pairs={{0,1},{1,2},{2,3},{3,4},{4,5},{5,6},{6,7},{8,9},{9,10},{10,11},{11... | collective-permute-start | bytes 786440 | tf_op jit(solution)/shard_map/ppermute | solution.py:22
  411.0 16.3 %collective-permute-start.39 = (f32[1,512,128]{2,1,0:T(8,128)}, f32[1,512,128]{2,1,0:T(8,128)}, u32[]{:S(2)}, u32[]{:S(2)}) collective-permute-start(f32[1,512,128]{2,1,0:T(8,128)} %get-tuple-element.91), channel_id=1, source_target_pairs={{1,0},{2,1},{3,2},{4,3},{5,4},{6,5},{7,6},{9,8},{10,9},{11,10},{12... | collective-permute-start | bytes 786440 | tf_op jit(solution)/shard_map/ppermute | solution.py:22
  (43 other events, 382.7 us)
